TPU v7x, 128 devices: a whole 4x4x4 slice. The times are simulated.
128 devices in a mesh: dp: 32 (over x, y, core), fsdp: 4 (over z).
Axes of the slice: x: 4, y: 4, z: 4, core: 2. Of those that a mesh axis runs over, the one named last changes fastest.
Arguments:
- tokens: bfloat16 [65536, 4608], P(('dp', 'fsdp')), as said below
- rmsnorm_gain_vector: bfloat16 [4608], replicated, may hold values from 0.099609375 to 1.8984375
- tied_query_matrix: bfloat16 [4608, 2048], P('fsdp'), may hold values from -0.09375 to 0.09375
- adapter_down_matrix: bfloat16 [4608, 128], P('fsdp'), may hold values from -0.09375 to 0.09375
- adapter_up_matrix: bfloat16 [128, 2048], replicated, may hold values from -0.5 to 0.5
- depth: int32 [4096], P(('dp', 'fsdp')), may hold values from 1 to 3, as said below
- destination: int32 [4096], P(('dp', 'fsdp')), may hold values from 0 to 31, as said below
- cotangent: bfloat16 [32768, 2048], P(('dp', 'fsdp')), may hold values from -6 to 6
Outputs:
- query: bfloat16 [32768, 2048], P(('dp', 'fsdp'))
- grad_tokens: bfloat16 [65536, 4608], P(('dp', 'fsdp'))
- grad_down: float32 [4608, 128], replicated
- grad_up: float32 [128, 2048], replicated
Inputs may be any that keep to these rules, and one draw needn't show every extreme that they name: Blocks that stop before this recursion have depth 1; the others have depth 2 or 3. `destination`: only entries of surviving blocks are read. Each dp index is named by exactly 16 surviving blocks with its own fsdp index, and by at most 1 surviving blocks of any one device; both bounds are reached in every draw. `tokens`: float values of mixed row and feature scales.
All inputs are finite; a program needn't handle non-finite values.
Results may differ from a plain program's by a relative error of at most 0.0053.
Values may be sent and summed in bfloat16 or wider, within the bound.
No kernel may reach another device: no remote copies, remote signals or barrier semaphores. Data moves between devices by JAX's collectives and lax.ppermute only.
A program may use at most 128 MiB of HBM per device.

v0:
```python
import jax
import jax.numpy as jnp
from jax import lax
from jax.sharding import Mesh, PartitionSpec as P

DP = ("x", "y", "core")
BF16 = jnp.bfloat16
F32 = jnp.float32


def dot(a, b, dims=((1,), (0,))):
    return lax.dot_general(a, b, (dims, ((), ())), preferred_element_type=F32)


def gather_down(down):
    me = lax.axis_index("fsdp")
    rows = down.shape[0]
    full = jnp.zeros((4 * rows, down.shape[1]), down.dtype)
    for step in range(4):
        part = down
        if step:
            part = lax.ppermute(down, "fsdp", [((i + step) % 4, i) for i in range(4)])
        full = lax.dynamic_update_slice(full, part, ((me + step) % 4 * rows, 0))
    return full


def gather_weight(weight):
    chip = lax.axis_index("x") * 4 + lax.axis_index("y")
    half = weight.shape[1] // 2
    rows = weight.shape[0] // 16
    piece = lax.dynamic_slice(weight, (chip * rows, lax.axis_index("core") * half), (rows, half))
    both = lax.all_gather(piece, ("core", "fsdp", "x", "y"), axis=0, tiled=True)
    return both.reshape(2, both.shape[0] // 2, half)


def reduce_gradients(grads):
    rows, lanes = grads.shape
    parts = lax.all_to_all(grads.astype(BF16), DP, 0, 0, tiled=True)
    mine = jnp.sum(parts.reshape(32, rows // 32, lanes).astype(F32), axis=0)
    mine = lax.psum(mine, "fsdp")
    return lax.all_gather(mine, DP, axis=0, tiled=True)


def body(tokens, gain, weight, down, up, depth, destination, cotangent):
    blocks = depth.shape[0]
    rows, width = tokens.shape
    block_rows = rows // blocks
    features = cotangent.shape[1]
    capacity = cotangent.shape[0] // block_rows
    live = depth >= 2
    dest = jnp.clip(destination, 0, 31)
    hit = live[None, :] & (dest[None, :] == jnp.arange(32, dtype=jnp.int32)[:, None])
    order = jnp.arange(blocks, dtype=jnp.int32)
    source = jnp.sum(jnp.where(hit, order[None, :], 0), axis=1)
    sent = jnp.any(hit, axis=1).astype(jnp.int32)
    flags = lax.all_to_all(sent, DP, 0, 0, tiled=True)
    rank = jnp.sum(jnp.where(order[None, :] < order[:, None], flags[None, :], 0), axis=1)
    seat = jnp.clip(rank, 0, capacity - 1)
    seats = jnp.arange(capacity, dtype=jnp.int32)
    match = (flags[None, :] > 0) & (rank[None, :] == seats[:, None])
    pick = jnp.sum(jnp.where(match, order[None, :], 0), axis=1)
    full_weight = gather_weight(weight)
    full_down = gather_down(down)
    g_send = jnp.take(cotangent.reshape(capacity, block_rows, features), seat, axis=0)
    g_got = lax.all_to_all(g_send, DP, 0, 0, tiled=True)
    g = jnp.where(live[:, None, None], jnp.take(g_got, dest, axis=0), jnp.zeros((), BF16))
    g = g.reshape(rows, features)
    x = tokens.astype(F32)
    inverse = lax.rsqrt(jnp.mean(x * x, axis=-1, keepdims=True) + 1e-06)
    gain_f = gain.astype(F32)
    xn = (x * inverse * gain_f).astype(BF16)
    low = dot(xn, full_down).astype(BF16)
    dlow = dot(g, up, ((1,), (1,))).astype(BF16)
    grad_up = dot(low, g, ((0,), (0,)))
    grad_down = dot(xn, dlow, ((0,), (0,)))
    grads = jnp.concatenate([grad_down, grad_up.reshape(-1, grad_down.shape[1])], axis=0)
    grads = reduce_gradients(grads)
    grad_down, grad_up = (grads[:width], grads[width:].reshape(grad_up.shape))
    half = features // 2
    q = jnp.concatenate([dot(xn, full_weight[0]), dot(xn, full_weight[1])], axis=1)
    q = (q + dot(low, up)).astype(BF16).reshape(blocks, block_rows, features)
    q_got = lax.all_to_all(jnp.take(q, source, axis=0), DP, 0, 0, tiled=True)
    query = jnp.take(q_got, pick, axis=0).reshape(capacity * block_rows, features)
    dxn = dot(g[:, :half], full_weight[0], ((1,), (1,))) + dot(
        g[:, half:], full_weight[1], ((1,), (1,))
    )
    dxn = dxn + dot(dlow, full_down, ((1,), (1,)))
    dy = dxn * gain_f
    normed = x * inverse
    grad_tokens = inverse * (dy - normed * jnp.mean(dy * normed, axis=-1, keepdims=True))
    grad_tokens = jnp.where(jnp.repeat(live, block_rows)[:, None], grad_tokens, 0.0).astype(BF16)
    return (query, grad_tokens, grad_down, grad_up)


def solution(mesh):
    fine = Mesh(mesh.devices.reshape(4, 4, 2, 4), ("x", "y", "core", "fsdp"))
    split = P(("x", "y", "core", "fsdp"))
    in_specs = (split, P(), P("fsdp"), P("fsdp"), P(), split, split, split)
    return jax.shard_map(
        body, mesh=fine, in_specs=in_specs, out_specs=(split, split, P(), P()), check_vma=False
    )
```

profile of v0, /device:TPU:1, one launch (start us, length us, event | category | flops | bytes accessed | tf_op | source)
XLA Modules:
  0.0 356.4 jit_solution(17156562937202370914)
XLA Ops:
  7.2 4.7 %collective-permute-start = (bf16[1152,128]{1,0:T(8,128)(2,1)}, bf16[1152,128]{1,0:T(8,128)(2,1)}, u32[]{:S(2)}, u32[]{:S(2)}) collective-permute-start(bf16[1152,128]{1,0:T(8,128)(2,1)} %param.13), channel_id=1, source_target_pairs={{1,0},{2,1},{3,2},{0,3},{5,4},{6,5},{7,6},{4,7},{9,8},{10,9},{11,1... | collective-permute-start | bytes 884744 | tf_op jit(solution)/shard_map/ppermute | solution.py:22
  11.9 0.7 collective-permute-start.2
  12.5 0.7 broadcast_compare_fusion.1
  13.2 0.7 broadcast_clamp_fusion
  14.0 0.7 copy.14
  14.7 8.6 %all-to-all-start = ((s32[32,1,1]{2,1,0:T(1,128)}), s32[32,1,1]{2,1,0:T(1,128)S(1)}, u32[]{:S(2)}, u32[]{:S(2)}) async-start(s32[32,1,1]{2,1,0:T(1,128)} %copy.14), calls=%async_computation | async-start | bytes 32768 | tf_op jit(solution)/shard_map/all_to_all | solution.py:56
  23.4 3.3 fusion.9
  26.7 3.4 all-to-all-done
  30.2 0.7 reduce
  31.0 0.7 gather_fusion.1
  31.7 1.6 broadcast_select_fusion.1
  33.3 4.3 %all-to-all-start.2 = ((bf16[32,16,2048]{2,1,0:T(8,128)(2,1)}), bf16[32,16,2048]{2,1,0:T(8,128)(2,1)S(1)}, u32[]{:S(2)}, u32[]{:S(2)}) async-start(bf16[32,16,2048]{2,1,0:T(8,128)(2,1)} %broadcast_select_fusion.1), calls=%async_computation.2 | async-start | bytes 4194304 | tf_op jit(solution)/shard_map/all_to_all | solution.py:65
  37.7 0.2 broadcast_in_dim.116
  38.0 1.0 constant_dynamic-update-slice_fusion.2
  39.0 1.0 constant_dynamic-update-slice_fusion.1
  40.1 1.0 copy-done.2
  41.1 3.8 %convolution_convert_fusion.3 = bf16[512,128]{1,0:T(8,128)(2,1)S(1)} fusion(bf16[4608,128]{1,0:T(8,128)(2,1)S(1)} %constant_dynamic-update-slice_fusion, bf16[512,4608]{1,0:T(8,128)(2,1)} %param.10, f32[4608]{0:T(1024)S(1)} %convert_element_type.45, f32[512]{0:T(512)S(1)} %add_rsqrt_fusion), kind=kOutput, calls=%fused_computation.35 | convolution fusion | flops 613482496 | bytes 6049792 | tf_op jit(solution)/shard_map/dot_general | solution.py:12
  44.9 21.1 %all-to-all-done.2 = bf16[32,16,2048]{2,1,0:T(8,128)(2,1)S(1)} async-done(((bf16[32,16,2048]{2,1,0:T(8,128)(2,1)}), bf16[32,16,2048]{2,1,0:T(8,128)(2,1)S(1)}, u32[]{:S(2)}, u32[]{:S(2)}) %all-to-all-start.2) | async-done | bytes 2097184 | tf_op jit(solution)/shard_map/all_to_all | solution.py:65
  66.0 2.0 gather_fusion.3
  68.0 1.9 select_select_fusion
  69.9 0.7 convolution_convert_fusion.2
  70.7 0.5 convolution_convert_fusion.1
  71.1 0.2 reshape.125
  71.4 4.1 %convolution_convert_fusion = bf16[4608,128]{1,0:T(8,128)(2,1)S(1)} fusion(bf16[512,128]{1,0:T(8,128)(2,1)S(1)} %convolution_convert_fusion.2, bf16[512,4608]{1,0:T(8,128)(2,1)} %param.10, f32[4608]{0:T(1024)S(1)} %convert_element_type.45, f32[512]{0:T(512)S(1)} %add_rsqrt_fusion), kind=kOutput, calls=%fused_computation.25 | convolution fusion | flops 614006784 | bytes 6049792 | tf_op jit(solution)/shard_map/dot_general | solution.py:12
  75.6 27.8 %all_to_all.25 = bf16[32,208,128]{2,1,0:T(8,128)(2,1)S(1)} all-to-all(bf16[32,208,128]{2,1,0:T(8,128)(2,1)S(1)} %bitcast.34), channel_id=1, replica_groups=mesh['x'=4,'y'=4,'core'=2,'fsdp'=4] {'x','y','core'}, dimensions={0} | all-to-all | bytes 3407872 | tf_op jit(solution)/shard_map/all_to_all | solution.py:38
  103.4 0.9 convert_reduce_fusion
  104.4 35.0 %all-reduce.2.cloned.1.call-done = f32[208,128]{1,0:T(8,128)} async-done(((f32[208,128]{1,0:T(8,128)}), f32[208,128]{1,0:T(8,128)}) %all-reduce.2.cloned.1.call-update) | async-done | bytes 106512 | tf_op jit(solution)/shard_map/psum | solution.py:40
  139.3 0.2 all-gather.3.cloned.1.call-start
  139.6 1.6 dynamic_slice.3
  141.5 0.1 select_reduce_fusion.2
  141.8 48.4 %all-gather.5.cloned.1.call-done = f32[6656,128]{1,0:T(8,128)} async-done(((f32[208,128]{1,0:T(8,128)}), f32[6656,128]{1,0:T(8,128)}) %all-gather.5.cloned.1.call-update) | async-done | bytes 3407888 | tf_op jit(solution)/shard_map/all_gather | solution.py:41
  190.2 1.3 slice.41
  191.5 1.1 reshape.126
  192.6 3.2 slice.40
  195.9 81.2 %all-gather.3.cloned.1.call-done = bf16[9216,1024]{1,0:T(8,128)(2,1)} async-done(((bf16[72,1024]{1,0:T(8,128)(2,1)}), bf16[9216,1024]{1,0:T(8,128)(2,1)}) %all-gather.3.cloned.1.call-update) | async-done | bytes 18874384 | tf_op jit(solution)/shard_map/all_gather | solution.py:32
  277.0 9.2 %fusion.12 = f32[512,1024]{1,0:T(8,128)S(1)} fusion(bf16[9216,1024]{1,0:T(8,128)(2,1)} %all-gather.3.cloned.1.call-done, bf16[512,4608]{1,0:T(8,128)(2,1)} %param.10, f32[4608]{0:T(1024)S(1)} %convert_element_type.45, f32[512]{0:T(512)S(1)} %add_rsqrt_fusion), kind=kOutput, calls=%fused_computation.19 | convolution fusion | flops 4841275392 | bytes 16273408 | tf_op jit(solution)/shard_map/dot_general | solution.py:12
  286.3 1.2 copy-done.8
  287.5 7.3 %fusion.16 = f32[512,1024]{1,0:T(8,128)S(1)} fusion(bf16[9216,1024]{1,0:T(8,128)(2,1)S(1)} %copy-done.8, bf16[512,4608]{1,0:T(8,128)(2,1)} %param.10, f32[4608]{0:T(1024)S(1)} %convert_element_type.45, f32[512]{0:T(512)S(1)} %add_rsqrt_fusion), kind=kOutput, calls=%fused_computation.23 | convolution fusion | flops 4841275392 | bytes 16275456 | tf_op jit(solution)/shard_map/dot_general | solution.py:12
  294.8 2.0 fusion.18
  296.9 3.6 %gather_fusion.2 = bf16[32,16,2048]{2,1,0:T(8,128)(2,1)} fusion(bf16[32,16,2048]{2,1,0:T(8,128)(2,1)} %bitcast.33, s32[1024]{0:T(1024)S(1)} %pad_clamp_fusion.3), kind=kCustom, calls=%fused_computation.clone | custom fusion | bytes 4194432 | tf_op jit(solution)/shard_map/jit(_take)/gather | solution.py:82
  300.4 3.2 broadcast_select_fusion
  303.6 7.2 %all-to-all-start.1 = ((bf16[32,16,2048]{2,1,0:T(8,128)(2,1)}), bf16[32,16,2048]{2,1,0:T(8,128)(2,1)}, u32[]{:S(2)}, u32[]{:S(2)}) async-start(bf16[32,16,2048]{2,1,0:T(8,128)(2,1)} %broadcast_select_fusion), calls=%async_computation.1 | async-start | bytes 4194304 | tf_op jit(solution)/shard_map/all_to_all | solution.py:82
  310.8 11.4 %fusion.10 = f32[512,4608]{1,0:T(8,128)} fusion(bf16[9216,1024]{1,0:T(8,128)(2,1)} %all-gather.3.cloned.1.call-done, bf16[512,2048]{1,0:T(8,128)(2,1)S(1)} %bitcast.31), kind=kOutput, calls=%fused_computation.17 | convolution fusion | flops 4831838208 | bytes 19922944 | tf_op jit(solution)/shard_map/dot_general | solution.py:12
  322.2 11.3 %fusion.14 = f32[512,4608]{1,0:T(8,128)} fusion(bf16[9216,1024]{1,0:T(8,128)(2,1)} %all-gather.3.cloned.1.call-done, bf16[512,2048]{1,0:T(8,128)(2,1)S(1)} %bitcast.32), kind=kOutput, calls=%fused_computation.21 | convolution fusion | flops 4831838208 | bytes 19922944 | tf_op jit(solution)/shard_map/dot_general | solution.py:12
  333.5 8.1 %fusion.4 = (f32[512]{0:T(512)S(1)}, f32[512,4608]{1,0:T(8,128)S(1)}) fusion(bf16[512,4608]{1,0:T(8,128)(2,1)S(1)} %bitcast.28, f32[512]{0:T(512)S(1)} %add_rsqrt_fusion, f32[4608]{0:T(1024)S(1)} %convert_element_type.45, bf16[512,128]{1,0:T(8,128)(2,1)S(1)} %convolution_convert_fusion.2, bf16[4608,128]{1,0:T(8,128)(2,1)S(1)} %copy-done.3, ...), kind=kOutput, calls=%fused_computation.10 | convolution fusion | flops 620494336 | bytes 34363392 | tf_op jit(solution)/shard_map/dot_general | solution.py:12
  341.6 4.8 %fusion.8 = bf16[512,4608]{1,0:T(8,128)(2,1)} fusion(f32[512,4608]{1,0:T(8,128)S(1)} %get-tuple-element.8, bf16[512,4608]{1,0:T(8,128)(2,1)S(1)} %bitcast.28, f32[512]{0:T(512)S(1)} %broadcast_multiply_fusion, f32[512]{0:T(512)S(1)} %add_rsqrt_fusion, pred[512]{0:T(512)(128)(4,1)S(1)} %broadcast_in_dim.119), kind=kLoop, calls=%fused_computation.14 | loop fusion | flops 16515072 | bytes 18878976 | tf_op jit(solution)/shard_map/convert_element_type | solution.py:91
  346.5 2.2 gather_fusion
  348.7 1.2 bitcast_select_fusion
  (59 shorter events, 1.2 us)
Async XLA Ops:
  7.2 23.8 %copy-start = (bf16[256,2048]{1,0:T(8,128)(2,1)S(1)}, bf16[256,2048]{1,0:T(8,128)(2,1)}, u32[]{:S(2)}) copy-start(bf16[256,2048]{1,0:T(8,128)(2,1)} %param.17) | copy-start | bytes 3145732
  7.2 19.5 %copy-start.7 = (bf16[4608]{0:T(1024)(128)(2,1)S(1)}, bf16[4608]{0:T(1024)(128)(2,1)}, u32[]{:S(2)}) copy-start(bf16[4608]{0:T(1024)(128)(2,1)} %param.11) | copy-start | bytes 27652
  7.2 30.8 %collective-permute-start = (bf16[1152,128]{1,0:T(8,128)(2,1)}, bf16[1152,128]{1,0:T(8,128)(2,1)}, u32[]{:S(2)}, u32[]{:S(2)}) collective-permute-start(bf16[1152,128]{1,0:T(8,128)(2,1)} %param.13), channel_id=1, source_target_pairs={{1,0},{2,1},{3,2},{0,3},{5,4},{6,5},{7,6},{4,7},{9,8},{10,9},{11,1... | collective-permute-start | bytes 884744 | tf_op jit(solution)/shard_map/ppermute | solution.py:22
  11.8 27.1 %collective-permute-start.1 = (bf16[1152,128]{1,0:T(8,128)(2,1)}, bf16[1152,128]{1,0:T(8,128)(2,1)}, u32[]{:S(2)}, u32[]{:S(2)}) collective-permute-start(bf16[1152,128]{1,0:T(8,128)(2,1)} %param.13), channel_id=1, source_target_pairs={{2,0},{3,1},{0,2},{1,3},{6,4},{7,5},{4,6},{5,7},{10,8},{11,9},{8,1... | collective-permute-start | bytes 884744 | tf_op jit(solution)/shard_map/ppermute | solution.py:22
  11.9 28.1 %collective-permute-start.2 = (bf16[1152,128]{1,0:T(8,128)(2,1)}, bf16[1152,128]{1,0:T(8,128)(2,1)S(1)}, u32[]{:S(2)}, u32[]{:S(2)}) collective-permute-start(bf16[1152,128]{1,0:T(8,128)(2,1)} %param.13), channel_id=1, source_target_pairs={{3,0},{0,1},{1,2},{2,3},{7,4},{4,5},{5,6},{6,7},{11,8},{8,9},{9,10... | collective-permute-start | bytes 884744 | tf_op jit(solution)/shard_map/ppermute | solution.py:22
  14.7 15.5 %all-to-all-start = ((s32[32,1,1]{2,1,0:T(1,128)}), s32[32,1,1]{2,1,0:T(1,128)S(1)}, u32[]{:S(2)}, u32[]{:S(2)}) async-start(s32[32,1,1]{2,1,0:T(1,128)} %copy.14), calls=%async_computation | async-start | bytes 32768 | tf_op jit(solution)/shard_map/all_to_all | solution.py:56
  31.7 6.2 %copy-start.6 = (bf16[1152,128]{1,0:T(8,128)(2,1)S(1)}, bf16[1152,128]{1,0:T(8,128)(2,1)}, u32[]{:S(2)}) copy-start(bf16[1152,128]{1,0:T(8,128)(2,1)} %param.13) | copy-start | bytes 884740
  31.7 6.2 %copy-start.9 = (s32[32]{0:T(128)S(1)}, s32[32]{0:T(128)}, u32[]{:S(2)}) copy-start(s32[32]{0:T(128)} %param.16) | copy-start | bytes 388
  33.3 32.7 %all-to-all-start.2 = ((bf16[32,16,2048]{2,1,0:T(8,128)(2,1)}), bf16[32,16,2048]{2,1,0:T(8,128)(2,1)S(1)}, u32[]{:S(2)}, u32[]{:S(2)}) async-start(bf16[32,16,2048]{2,1,0:T(8,128)(2,1)} %broadcast_select_fusion.1), calls=%async_computation.2 | async-start | bytes 4194304 | tf_op jit(solution)/shard_map/all_to_all | solution.py:65
  37.6 101.7 %all-reduce.2.cloned.1.call-start = ((), (), s32[]{:S(2)}) async-start(), calls=%async_computation.5 | async-start | bytes 212992 | tf_op jit(solution)/shard_map/psum | solution.py:40
  40.0 1.0 copy-start.2
  44.8 25.1 %copy-start.4 = (bf16[128,2048]{1,0:T(8,128)(2,1)S(1)}, bf16[128,2048]{1,0:T(8,128)(2,1)}, u32[]{:S(2)}) copy-start(bf16[128,2048]{1,0:T(8,128)(2,1)} %param.14) | copy-start | bytes 1572868
  104.3 85.9 %all-gather.5.cloned.1.call-start = ((), (), s32[]{:S(2)}) async-start(), calls=%async_computation.6 | async-start | bytes 3514368 | tf_op jit(solution)/shard_map/all_gather | solution.py:41
  139.3 137.7 %all-gather.3.cloned.1.call-start = ((), (), s32[]{:S(2)}) async-start(), calls=%async_computation.4 | async-start | bytes 19021824 | tf_op jit(solution)/shard_map/all_gather | solution.py:32
  277.0 10.5 %copy-start.8 = (bf16[9216,1024]{1,0:T(8,128)(2,1)S(1)}, bf16[9216,1024]{1,0:T(8,128)(2,1)}, u32[]{:S(2)}) copy-start(bf16[9216,1024]{1,0:T(8,128)(2,1)} %all-gather.3.cloned.1.call-done) | copy-start | bytes 56623108
  287.5 7.3 %copy-start.5 = (bf16[128,2048]{1,0:T(8,128)(2,1)S(1)}, bf16[128,2048]{1,0:T(8,128)(2,1)}, u32[]{:S(2)}) copy-start(bf16[128,2048]{1,0:T(8,128)(2,1)} %param.14) | copy-start | bytes 1572868
  303.6 42.9 %all-to-all-start.1 = ((bf16[32,16,2048]{2,1,0:T(8,128)(2,1)}), bf16[32,16,2048]{2,1,0:T(8,128)(2,1)}, u32[]{:S(2)}, u32[]{:S(2)}) async-start(bf16[32,16,2048]{2,1,0:T(8,128)(2,1)} %broadcast_select_fusion), calls=%async_computation.1 | async-start | bytes 4194304 | tf_op jit(solution)/shard_map/all_to_all | solution.py:82
  310.8 22.7 %slice-start = ((s8[4718592]{0:T(1024)(128)(4,1)}), s8[4194304]{0:T(1024)(128)(4,1)S(1)}, s32[]{:S(2)}) async-start(s8[4718592]{0:T(1024)(128)(4,1)} %bitcast.27), calls=%async_computation.7 | async-start | bytes 8388608
  322.2 11.3 %slice-start.1 = ((s8[4718592]{0:T(1024)(128)(4,1)}), s8[524288]{0:T(1024)(128)(4,1)S(1)}, s32[]{:S(2)}) async-start(s8[4718592]{0:T(1024)(128)(4,1)} %bitcast.27), calls=%async_computation.8 | async-start | bytes 1048576
  322.2 11.3 %copy-start.3 = (bf16[4608,128]{1,0:T(8,128)(2,1)S(1)}, bf16[4608,128]{1,0:T(8,128)(2,1)}, u32[]{:S(2)}) copy-start(bf16[4608,128]{1,0:T(8,128)(2,1)} %copy-done.2) | copy-start | bytes 3538948
  341.6 8.2 %copy-start.1 = (bf16[256,2048]{1,0:T(8,128)(2,1)S(1)}, bf16[256,2048]{1,0:T(8,128)(2,1)}, u32[]{:S(2)}) copy-start(bf16[256,2048]{1,0:T(8,128)(2,1)} %param.17) | copy-start | bytes 3145732
Sparse Core Ops, SparseCore 0:
  104.4 34.8 all-reduce.1
  141.8 48.3 all-gather.4
  194.2 82.7 all-gather.2
where the time goes:
time: 357 us; the launch traced here: 356 us
  waiting for transfers between devices  189 us (53%)
  matrix products  58.4 us (16%)
  blocking collectives  27.8 us (8%)
  starting transfers between devices  25.7 us (7%)
  local copies, waits for them, and re-layouts  21.6 us (6%)
  other arithmetic  19.5 us (5%)
  between operations  14.2 us (4%)
    all_gather x1, waiting for transfers between devices, gather_weight(): both = lax.all_gather(piece, ('core', 'fsdp', 'x', 'y'), axis=0, tiled=True)  81.2 us
    dot_general x10, matrix products, dot(): return lax.dot_general(a, b, (dims, ((), ())), preferred_element_type=F32)  58.4 us
    all_gather x1, waiting for transfers between devices, reduce_gradients(): return lax.all_gather(mine, DP, axis=0, tiled=True)  48.4 us
    psum x1, waiting for transfers between devices, reduce_gradients(): mine = lax.psum(mine, 'fsdp')  35 us
    all_to_all x1, blocking collectives, reduce_gradients(): parts = lax.all_to_all(grads.astype(BF16), DP, 0, 0, tiled=True)  27.8 us
    all_to_all x1, waiting for transfers between devices, body(): g_got = lax.all_to_all(g_send, DP, 0, 0, tiled=True)  21.1 us
    all_to_all x1, starting transfers between devices, body(): flags = lax.all_to_all(sent, DP, 0, 0, tiled=True)  8.6 us
    all_to_all x1, starting transfers between devices, body(): q_got = lax.all_to_all(jnp.take(q, source, axis=0), DP, 0, 0, tiled=True)  7.17 us
  transfers between devices with their start and end apart: 9, of which 5 were waited for; matrix products, arithmetic and copies ran while one was open for 16% of the time, Pallas kernels for 0%

commit v1 on v0

--- a/solution.py
+++ b/solution.py
@@ -6,6 +6,14 @@
 DP = ("x", "y", "core")
 BF16 = jnp.bfloat16
 F32 = jnp.float32
+
+
+def process_map(sample):
+    v1 = jax.lax.psum(1, DP)
+    aux = jnp.stack(v1 * [sample], 0)
+    earlier = jax.lax.all_to_all(aux, DP, 0, 0)
+    high = jnp.concatenate(earlier, 0)
+    return high
 
 
 def dot(a, b, dims=((1,), (0,))):
@@ -38,7 +46,7 @@
     parts = lax.all_to_all(grads.astype(BF16), DP, 0, 0, tiled=True)
     mine = jnp.sum(parts.reshape(32, rows // 32, lanes).astype(F32), axis=0)
     mine = lax.psum(mine, "fsdp")
-    return lax.all_gather(mine, DP, axis=0, tiled=True)
+    return process_map(mine)
 
 
 def body(tokens, gain, weight, down, up, depth, destination, cotangent):

time: 357 us -> 304 us (0.85)
  waiting for transfers between devices: 189 us -> 123 us
  starting transfers between devices: 25.7 us -> 34 us
    all_gather x1, waiting for transfers between devices: 81.2 us -> 0.01 us  [gather_weight(): both = lax.all_gather(piece, ('core', 'fsdp', 'x', 'y'), axis=0, tiled=True)]
    all_to_all x0 -> x1, waiting for transfers between devices: none -> 65.5 us  [process_map(): earlier = jax.lax.all_to_all(aux, DP, 0, 0)]
    all_gather x1 -> x0, waiting for transfers between devices: 48.4 us -> none  [reduce_gradients(): return lax.all_gather(mine, DP, axis=0, tiled=True)]
    all_to_all x0 -> x1, starting transfers between devices: none -> 10.3 us  [process_map(): earlier = jax.lax.all_to_all(aux, DP, 0, 0)]
  transfers between devices with their start and end apart: 9 -> 9, of which waited for: 5 -> 4; matrix products, arithmetic and copies ran while one was open for 16% -> 20% of each run, Pallas kernels for 0% -> 0%
where the time goes in v1:
time: 304 us
  waiting for transfers between devices  123 us (40%)
  matrix products  58.4 us (19%)
  starting transfers between devices  34 us (11%)
  blocking collectives  27.8 us (9%)
  local copies, waits for them, and re-layouts  24.4 us (8%)
  other arithmetic  19.5 us (6%)
  between operations  16 us (5%)
    all_to_all x1, waiting for transfers between devices, process_map(): earlier = jax.lax.all_to_all(aux, DP, 0, 0)  65.5 us
    dot_general x10, matrix products, dot(): return lax.dot_general(a, b, (dims, ((), ())), preferred_element_type=F32)  58.4 us
    psum x1, waiting for transfers between devices, reduce_gradients(): mine = lax.psum(mine, 'fsdp')  33.3 us
    all_to_all x1, blocking collectives, reduce_gradients(): parts = lax.all_to_all(grads.astype(BF16), DP, 0, 0, tiled=True)  27.8 us
    all_to_all x1, waiting for transfers between devices, body(): g_got = lax.all_to_all(g_send, DP, 0, 0, tiled=True)  21.1 us
    all_to_all x1, starting transfers between devices, process_map(): earlier = jax.lax.all_to_all(aux, DP, 0, 0)  10.3 us
    all_to_all x1, starting transfers between devices, body(): flags = lax.all_to_all(sent, DP, 0, 0, tiled=True)  8.6 us
  transfers between devices with their start and end apart: 9, of which 4 were waited for; matrix products, arithmetic and copies ran while one was open for 20% of the time, Pallas kernels for 0%

profile of v1, /device:TPU:1, one launch (start us, length us, event | category | flops | bytes accessed | tf_op | source)
XLA Modules:
  0.0 303.6 jit_solution(13751810822933519023)
XLA Ops:
  8.0 4.7 %collective-permute-start = (bf16[1152,128]{1,0:T(8,128)(2,1)}, bf16[1152,128]{1,0:T(8,128)(2,1)}, u32[]{:S(2)}, u32[]{:S(2)}) collective-permute-start(bf16[1152,128]{1,0:T(8,128)(2,1)} %param.13), channel_id=1, source_target_pairs={{1,0},{2,1},{3,2},{0,3},{5,4},{6,5},{7,6},{4,7},{9,8},{10,9},{11,1... | collective-permute-start | bytes 884744 | tf_op jit(solution)/shard_map/ppermute | solution.py:30
  12.7 0.7 collective-permute-start.2
  13.4 0.7 broadcast_compare_fusion.1
  14.0 0.7 broadcast_clamp_fusion
  14.8 0.7 copy.14
  15.5 8.6 %all-to-all-start = ((s32[32,1,1]{2,1,0:T(1,128)}), s32[32,1,1]{2,1,0:T(1,128)S(1)}, u32[]{:S(2)}, u32[]{:S(2)}) async-start(s32[32,1,1]{2,1,0:T(1,128)} %copy.14), calls=%async_computation | async-start | bytes 32768 | tf_op jit(solution)/shard_map/all_to_all | solution.py:64
  24.2 3.3 %fusion.9 = f32[512]{0:T(512)S(1)} fusion(bf16[512,4608]{1,0:T(8,128)(2,1)} %param.10), kind=kLoop, calls=%fused_computation.15 | loop fusion | flops 7077376 | bytes 4720640 | tf_op jit(solution)/shard_map/reduce_sum | solution.py:77
  27.6 3.4 %all-to-all-done = s32[32,1,1]{2,1,0:T(1,128)S(1)} async-done(((s32[32,1,1]{2,1,0:T(1,128)}), s32[32,1,1]{2,1,0:T(1,128)S(1)}, u32[]{:S(2)}, u32[]{:S(2)}) %all-to-all-start) | async-done | bytes 160 | tf_op jit(solution)/shard_map/all_to_all | solution.py:64
  31.0 0.7 reduce
  31.8 0.7 gather_fusion.1
  32.5 1.6 broadcast_select_fusion.1
  34.1 4.3 %all-to-all-start.2 = ((bf16[32,16,2048]{2,1,0:T(8,128)(2,1)}), bf16[32,16,2048]{2,1,0:T(8,128)(2,1)S(1)}, u32[]{:S(2)}, u32[]{:S(2)}) async-start(bf16[32,16,2048]{2,1,0:T(8,128)(2,1)} %broadcast_select_fusion.1), calls=%async_computation.2 | async-start | bytes 4194304 | tf_op jit(solution)/shard_map/all_to_all | solution.py:73
  38.5 0.2 broadcast_in_dim.116
  38.8 1.0 constant_dynamic-update-slice_fusion.2
  39.8 1.0 constant_dynamic-update-slice_fusion.1
  40.9 1.0 copy-done.2
  41.9 3.8 %convolution_convert_fusion.3 = bf16[512,128]{1,0:T(8,128)(2,1)S(1)} fusion(bf16[4608,128]{1,0:T(8,128)(2,1)S(1)} %constant_dynamic-update-slice_fusion, bf16[512,4608]{1,0:T(8,128)(2,1)} %param.10, f32[4608]{0:T(1024)S(1)} %convert_element_type.45, f32[512]{0:T(512)S(1)} %add_rsqrt_fusion), kind=kOutput, calls=%fused_computation.35 | convolution fusion | flops 613482496 | bytes 6049792 | tf_op jit(solution)/shard_map/dot_general | solution.py:20
  45.7 21.1 %all-to-all-done.2 = bf16[32,16,2048]{2,1,0:T(8,128)(2,1)S(1)} async-done(((bf16[32,16,2048]{2,1,0:T(8,128)(2,1)}), bf16[32,16,2048]{2,1,0:T(8,128)(2,1)S(1)}, u32[]{:S(2)}, u32[]{:S(2)}) %all-to-all-start.2) | async-done | bytes 2097184 | tf_op jit(solution)/shard_map/all_to_all | solution.py:73
  66.8 2.0 gather_fusion.3
  68.8 1.9 select_select_fusion
  70.8 0.7 convolution_convert_fusion.2
  71.5 0.5 convolution_convert_fusion.1
  72.0 0.2 reshape.130
  72.2 4.1 %convolution_convert_fusion = bf16[4608,128]{1,0:T(8,128)(2,1)S(1)} fusion(bf16[512,128]{1,0:T(8,128)(2,1)S(1)} %convolution_convert_fusion.2, bf16[512,4608]{1,0:T(8,128)(2,1)} %param.10, f32[4608]{0:T(1024)S(1)} %convert_element_type.45, f32[512]{0:T(512)S(1)} %add_rsqrt_fusion), kind=kOutput, calls=%fused_computation.25 | convolution fusion | flops 614006784 | bytes 6049792 | tf_op jit(solution)/shard_map/dot_general | solution.py:20
  76.4 27.8 %all_to_all.30 = bf16[32,208,128]{2,1,0:T(8,128)(2,1)S(1)} all-to-all(bf16[32,208,128]{2,1,0:T(8,128)(2,1)S(1)} %bitcast.35), channel_id=1, replica_groups=mesh['x'=4,'y'=4,'core'=2,'fsdp'=4] {'x','y','core'}, dimensions={0} | all-to-all | bytes 3407872 | tf_op jit(solution)/shard_map/all_to_all | solution.py:46
  104.2 0.9 convert_reduce_fusion
  105.2 1.6 dynamic_slice.3
  106.8 33.3 %all-reduce.2.cloned.1.call-done = f32[208,128]{1,0:T(8,128)} async-done(((f32[208,128]{1,0:T(8,128)}), f32[208,128]{1,0:T(8,128)}) %all-reduce.2.cloned.1.call-update) | async-done | bytes 106512 | tf_op jit(solution)/shard_map/psum | solution.py:48
  140.2 2.9 stack.2
  143.0 10.3 %all-to-all-start.4 = ((f32[32,208,128]{2,1,0:T(8,128)}), f32[32,208,128]{2,1,0:T(8,128)}, u32[]{:S(2)}, u32[]{:S(2)}) async-start(f32[32,208,128]{2,1,0:T(8,128)} %stack.2), calls=%async_computation.4 | async-start | bytes 6815744 | tf_op jit(solution)/shard_map/all_to_all | solution.py:14
  153.6 0.1 select_reduce_fusion.2
  153.9 65.5 %all-to-all-done.4 = f32[32,208,128]{2,1,0:T(8,128)} async-done(((f32[32,208,128]{2,1,0:T(8,128)}), f32[32,208,128]{2,1,0:T(8,128)}, u32[]{:S(2)}, u32[]{:S(2)}) %all-to-all-start.4) | async-done | bytes 3407904 | tf_op jit(solution)/shard_map/all_to_all | solution.py:14
  219.4 3.3 %slice.40 = f32[4608,128]{1,0:T(8,128)} slice(f32[6656,128]{1,0:T(8,128)} %bitcast.10), slice={[0:4608], [0:128]} | slice | bytes 4718592 | tf_op jit(solution)/shard_map/slice | solution.py:86
  222.7 1.3 slice.41
  224.0 1.1 reshape.132
  225.1 9.2 %fusion.12 = f32[512,1024]{1,0:T(8,128)S(1)} fusion(bf16[9216,1024]{1,0:T(8,128)(2,1)} %all-gather.2.cloned.1.call-done, bf16[512,4608]{1,0:T(8,128)(2,1)} %param.10, f32[4608]{0:T(1024)S(1)} %convert_element_type.45, f32[512]{0:T(512)S(1)} %add_rsqrt_fusion), kind=kOutput, calls=%fused_computation.19 | convolution fusion | flops 4841275392 | bytes 16273408 | tf_op jit(solution)/shard_map/dot_general | solution.py:20
  234.3 1.2 copy-done.8
  235.6 7.3 %fusion.16 = f32[512,1024]{1,0:T(8,128)S(1)} fusion(bf16[9216,1024]{1,0:T(8,128)(2,1)S(1)} %copy-done.8, bf16[512,4608]{1,0:T(8,128)(2,1)} %param.10, f32[4608]{0:T(1024)S(1)} %convert_element_type.45, f32[512]{0:T(512)S(1)} %add_rsqrt_fusion), kind=kOutput, calls=%fused_computation.23 | convolution fusion | flops 4841275392 | bytes 16275456 | tf_op jit(solution)/shard_map/dot_general | solution.py:20
  242.9 2.0 fusion.18
  244.9 3.6 %gather_fusion.2 = bf16[32,16,2048]{2,1,0:T(8,128)(2,1)} fusion(bf16[32,16,2048]{2,1,0:T(8,128)(2,1)} %bitcast.34, s32[1024]{0:T(1024)S(1)} %pad_clamp_fusion.3), kind=kCustom, calls=%fused_computation.clone | custom fusion | bytes 4194432 | tf_op jit(solution)/shard_map/jit(_take)/gather | solution.py:90
  248.5 3.2 %broadcast_select_fusion = bf16[32,16,2048]{2,1,0:T(8,128)(2,1)} fusion(bf16[32,16,2048]{2,1,0:T(8,128)(2,1)} %gather_fusion.2, pred[32]{0:T(512)(128)(4,1)S(1)} %compare_and_fusion.1), kind=kLoop, calls=%fused_computation.31 | loop fusion | flops 1048576 | bytes 4194336 | tf_op jit(solution)/shard_map/jit(_take)/select_n | solution.py:90
  251.7 5.4 %all-to-all-start.1 = ((bf16[32,16,2048]{2,1,0:T(8,128)(2,1)}), bf16[32,16,2048]{2,1,0:T(8,128)(2,1)}, u32[]{:S(2)}, u32[]{:S(2)}) async-start(bf16[32,16,2048]{2,1,0:T(8,128)(2,1)} %broadcast_select_fusion), calls=%async_computation.1 | async-start | bytes 4194304 | tf_op jit(solution)/shard_map/all_to_all | solution.py:90
  257.1 11.3 %fusion.10 = f32[512,4608]{1,0:T(8,128)} fusion(bf16[9216,1024]{1,0:T(8,128)(2,1)} %all-gather.2.cloned.1.call-done, bf16[512,2048]{1,0:T(8,128)(2,1)S(1)} %bitcast.32), kind=kOutput, calls=%fused_computation.17 | convolution fusion | flops 4831838208 | bytes 19922944 | tf_op jit(solution)/shard_map/dot_general | solution.py:20
  268.5 11.3 %fusion.14 = f32[512,4608]{1,0:T(8,128)} fusion(bf16[9216,1024]{1,0:T(8,128)(2,1)} %all-gather.2.cloned.1.call-done, bf16[512,2048]{1,0:T(8,128)(2,1)S(1)} %bitcast.33), kind=kOutput, calls=%fused_computation.21 | convolution fusion | flops 4831838208 | bytes 19922944 | tf_op jit(solution)/shard_map/dot_general | solution.py:20
  279.9 8.1 %fusion.4 = (f32[512]{0:T(512)S(1)}, f32[512,4608]{1,0:T(8,128)S(1)}) fusion(bf16[512,4608]{1,0:T(8,128)(2,1)S(1)} %bitcast.29, f32[512]{0:T(512)S(1)} %add_rsqrt_fusion, f32[4608]{0:T(1024)S(1)} %convert_element_type.45, bf16[512,128]{1,0:T(8,128)(2,1)S(1)} %convolution_convert_fusion.2, bf16[4608,128]{1,0:T(8,128)(2,1)S(1)} %copy-done.3, ...), kind=kOutput, calls=%fused_computation.10 | convolution fusion | flops 620494336 | bytes 34363392 | tf_op jit(solution)/shard_map/dot_general | solution.py:20
  288.0 4.8 %fusion.8 = bf16[512,4608]{1,0:T(8,128)(2,1)} fusion(f32[512,4608]{1,0:T(8,128)S(1)} %get-tuple-element.8, bf16[512,4608]{1,0:T(8,128)(2,1)S(1)} %bitcast.29, f32[512]{0:T(512)S(1)} %broadcast_multiply_fusion, f32[512]{0:T(512)S(1)} %add_rsqrt_fusion, pred[512]{0:T(512)(128)(4,1)S(1)} %broadcast_in_dim.119), kind=kLoop, calls=%fused_computation.14 | loop fusion | flops 16515072 | bytes 18878976 | tf_op jit(solution)/shard_map/convert_element_type | solution.py:99
  292.8 2.2 gather_fusion
  295.0 1.2 bitcast_select_fusion
  (59 shorter events, 1.2 us)
Async XLA Ops:
  8.0 23.8 %copy-start = (bf16[256,2048]{1,0:T(8,128)(2,1)S(1)}, bf16[256,2048]{1,0:T(8,128)(2,1)}, u32[]{:S(2)}) copy-start(bf16[256,2048]{1,0:T(8,128)(2,1)} %param.17) | copy-start | bytes 3145732
  8.0 19.5 %copy-start.7 = (bf16[4608]{0:T(1024)(128)(2,1)S(1)}, bf16[4608]{0:T(1024)(128)(2,1)}, u32[]{:S(2)}) copy-start(bf16[4608]{0:T(1024)(128)(2,1)} %param.11) | copy-start | bytes 27652
  8.0 30.8 %collective-permute-start = (bf16[1152,128]{1,0:T(8,128)(2,1)}, bf16[1152,128]{1,0:T(8,128)(2,1)}, u32[]{:S(2)}, u32[]{:S(2)}) collective-permute-start(bf16[1152,128]{1,0:T(8,128)(2,1)} %param.13), channel_id=1, source_target_pairs={{1,0},{2,1},{3,2},{0,3},{5,4},{6,5},{7,6},{4,7},{9,8},{10,9},{11,1... | collective-permute-start | bytes 884744 | tf_op jit(solution)/shard_map/ppermute | solution.py:30
  12.7 27.1 %collective-permute-start.1 = (bf16[1152,128]{1,0:T(8,128)(2,1)}, bf16[1152,128]{1,0:T(8,128)(2,1)}, u32[]{:S(2)}, u32[]{:S(2)}) collective-permute-start(bf16[1152,128]{1,0:T(8,128)(2,1)} %param.13), channel_id=1, source_target_pairs={{2,0},{3,1},{0,2},{1,3},{6,4},{7,5},{4,6},{5,7},{10,8},{11,9},{8,1... | collective-permute-start | bytes 884744 | tf_op jit(solution)/shard_map/ppermute | solution.py:30
  12.7 28.1 %collective-permute-start.2 = (bf16[1152,128]{1,0:T(8,128)(2,1)}, bf16[1152,128]{1,0:T(8,128)(2,1)S(1)}, u32[]{:S(2)}, u32[]{:S(2)}) collective-permute-start(bf16[1152,128]{1,0:T(8,128)(2,1)} %param.13), channel_id=1, source_target_pairs={{3,0},{0,1},{1,2},{2,3},{7,4},{4,5},{5,6},{6,7},{11,8},{8,9},{9,10... | collective-permute-start | bytes 884744 | tf_op jit(solution)/shard_map/ppermute | solution.py:30
  15.5 15.5 %all-to-all-start = ((s32[32,1,1]{2,1,0:T(1,128)}), s32[32,1,1]{2,1,0:T(1,128)S(1)}, u32[]{:S(2)}, u32[]{:S(2)}) async-start(s32[32,1,1]{2,1,0:T(1,128)} %copy.14), calls=%async_computation | async-start | bytes 32768 | tf_op jit(solution)/shard_map/all_to_all | solution.py:64
  32.5 6.2 %copy-start.6 = (bf16[1152,128]{1,0:T(8,128)(2,1)S(1)}, bf16[1152,128]{1,0:T(8,128)(2,1)}, u32[]{:S(2)}) copy-start(bf16[1152,128]{1,0:T(8,128)(2,1)} %param.13) | copy-start | bytes 884740
  32.5 6.2 %copy-start.9 = (s32[32]{0:T(128)S(1)}, s32[32]{0:T(128)}, u32[]{:S(2)}) copy-start(s32[32]{0:T(128)} %param.16) | copy-start | bytes 388
  34.1 32.7 %all-to-all-start.2 = ((bf16[32,16,2048]{2,1,0:T(8,128)(2,1)}), bf16[32,16,2048]{2,1,0:T(8,128)(2,1)S(1)}, u32[]{:S(2)}, u32[]{:S(2)}) async-start(bf16[32,16,2048]{2,1,0:T(8,128)(2,1)} %broadcast_select_fusion.1), calls=%async_computation.2 | async-start | bytes 4194304 | tf_op jit(solution)/shard_map/all_to_all | solution.py:73
  38.4 101.7 %all-reduce.2.cloned.1.call-start = ((), (), s32[]{:S(2)}) async-start(), calls=%async_computation.6 | async-start | bytes 212992 | tf_op jit(solution)/shard_map/psum | solution.py:48
  40.9 1.0 copy-start.2
  45.7 25.1 %copy-start.4 = (bf16[128,2048]{1,0:T(8,128)(2,1)S(1)}, bf16[128,2048]{1,0:T(8,128)(2,1)}, u32[]{:S(2)}) copy-start(bf16[128,2048]{1,0:T(8,128)(2,1)} %param.14) | copy-start | bytes 1572868
  105.1 120.0 %all-gather.2.cloned.1.call-start = ((), (), s32[]{:S(2)}) async-start(), calls=%async_computation.5 | async-start | bytes 19021824 | tf_op jit(solution)/shard_map/all_gather | solution.py:40
  143.0 76.4 %all-to-all-start.4 = ((f32[32,208,128]{2,1,0:T(8,128)}), f32[32,208,128]{2,1,0:T(8,128)}, u32[]{:S(2)}, u32[]{:S(2)}) async-start(f32[32,208,128]{2,1,0:T(8,128)} %stack.2), calls=%async_computation.4 | async-start | bytes 6815744 | tf_op jit(solution)/shard_map/all_to_all | solution.py:14
  225.1 10.5 %copy-start.8 = (bf16[9216,1024]{1,0:T(8,128)(2,1)S(1)}, bf16[9216,1024]{1,0:T(8,128)(2,1)}, u32[]{:S(2)}) copy-start(bf16[9216,1024]{1,0:T(8,128)(2,1)} %all-gather.2.cloned.1.call-done) | copy-start | bytes 56623108
  235.6 7.3 %copy-start.5 = (bf16[128,2048]{1,0:T(8,128)(2,1)S(1)}, bf16[128,2048]{1,0:T(8,128)(2,1)}, u32[]{:S(2)}) copy-start(bf16[128,2048]{1,0:T(8,128)(2,1)} %param.14) | copy-start | bytes 1572868
  251.7 41.1 %all-to-all-start.1 = ((bf16[32,16,2048]{2,1,0:T(8,128)(2,1)}), bf16[32,16,2048]{2,1,0:T(8,128)(2,1)}, u32[]{:S(2)}, u32[]{:S(2)}) async-start(bf16[32,16,2048]{2,1,0:T(8,128)(2,1)} %broadcast_select_fusion), calls=%async_computation.1 | async-start | bytes 4194304 | tf_op jit(solution)/shard_map/all_to_all | solution.py:90
  257.1 22.7 %slice-start = ((s8[4718592]{0:T(1024)(128)(4,1)}), s8[4194304]{0:T(1024)(128)(4,1)S(1)}, s32[]{:S(2)}) async-start(s8[4718592]{0:T(1024)(128)(4,1)} %bitcast.28), calls=%async_computation.7 | async-start | bytes 8388608
  268.5 11.4 %slice-start.1 = ((s8[4718592]{0:T(1024)(128)(4,1)}), s8[524288]{0:T(1024)(128)(4,1)S(1)}, s32[]{:S(2)}) async-start(s8[4718592]{0:T(1024)(128)(4,1)} %bitcast.28), calls=%async_computation.8 | async-start | bytes 1048576
  268.5 11.4 %copy-start.3 = (bf16[4608,128]{1,0:T(8,128)(2,1)S(1)}, bf16[4608,128]{1,0:T(8,128)(2,1)}, u32[]{:S(2)}) copy-start(bf16[4608,128]{1,0:T(8,128)(2,1)} %copy-done.2) | copy-start | bytes 3538948
  288.0 8.2 %copy-start.1 = (bf16[256,2048]{1,0:T(8,128)(2,1)S(1)}, bf16[256,2048]{1,0:T(8,128)(2,1)}, u32[]{:S(2)}) copy-start(bf16[256,2048]{1,0:T(8,128)(2,1)} %param.17) | copy-start | bytes 3145732
Sparse Core Ops, SparseCore 0:
  105.3 34.8 all-reduce.1
Sparse Core Ops, SparseCore 1:
  109.2 111.6 all-gather.1
